TPU v7x, 32 devices: a whole 2x2x4 slice. The times are simulated.
32 devices in a mesh: energy: 8 (over y, x, core), cell: 4 (over z).
Axes of the slice: x: 2, y: 2, z: 4, core: 2. Of those that a mesh axis runs over, the one named last changes fastest.
Arguments:
- retarded_diag: bfloat16 [2, 16, 16, 256, 256], P(None, 'energy', 'cell'), may hold values from -0.375 to 0.375
- retarded_lower: bfloat16 [2, 16, 16, 256, 256], P(None, 'energy', 'cell'), may hold values from -0.375 to 0.375
- retarded_upper: bfloat16 [2, 16, 16, 256, 256], P(None, 'energy', 'cell'), may hold values from -0.375 to 0.375
- sigma_lesser: bfloat16 [2, 16, 16, 256, 256], P(None, 'energy', 'cell'), may hold values from -6 to 6
- screened: bfloat16 [2, 16, 32], P(None, 'cell'), may hold values from -1 to 1
- kept: int32 [16, 8], P('cell'), may hold values from 0 to 15, as said below
- kept_count: int32 [16], P('cell'), may hold values from 1 to 8, as said below
Outputs:
- sigma_new: bfloat16 [2, 16, 16, 8, 4096], P(None, 'energy', 'cell')
Inputs may be any that keep to these rules, and one draw needn't show every extreme that they name: `kept`: each row holds 8 different sub-block numbers. `kept_count`: some cell has 8 live slots and some other cell 1.
All inputs are finite; a program needn't handle non-finite values.
Results may differ from a plain program's by a relative error of at most 0.0057.
Values may be sent and summed in bfloat16 or wider, within the bound.
No kernel may reach another device: no remote copies, remote signals or barrier semaphores. Data moves between devices by JAX's collectives and lax.ppermute only.
A program may use at most 128 MiB of HBM per device.

v0:
```python
from functools import partial

import jax
import jax.numpy as jnp
from jax import lax
from jax.sharding import PartitionSpec as P

ORB = 256
SUB = 64
KMAX = 8


def with_halo(block, sides, width):
    for axis, dim in sides:
        count = lax.axis_size(axis)
        forward = [(i, i + 1) for i in range(count - 1)]
        backward = [(target, source) for source, target in forward]
        low = lax.ppermute(
            lax.slice_in_dim(block, block.shape[dim] - width, None, axis=dim), axis, forward
        )
        high = lax.ppermute(lax.slice_in_dim(block, 0, width, axis=dim), axis, backward)
        block = jnp.concatenate([low, block, high], axis=dim)
    return block


def batched(left_side, right_side):
    return jnp.einsum("ecij,ecjk->ecik", left_side, right_side, preferred_element_type=jnp.float32)


def strips(hot, blocks):
    shaped = blocks.reshape(blocks.shape[0], blocks.shape[1], hot.shape[2], SUB, blocks.shape[3])
    return jnp.einsum("ckp,ecpij->eckij", hot, shaped, preferred_element_type=jnp.float32).astype(
        jnp.bfloat16
    )


def outer_part(left_side, right_side):
    return jnp.einsum(
        "eckij,eckqj->cekiq", left_side, right_side, preferred_element_type=jnp.float32
    )


def kept_sandwich(row_hot, col_hot, factor, middle):
    inner_r = (batched(factor[0], middle[0]) - batched(factor[1], middle[1])).astype(jnp.bfloat16)
    inner_i = (batched(factor[0], middle[1]) + batched(factor[1], middle[0])).astype(jnp.bfloat16)
    rows_r = strips(row_hot, inner_r)
    rows_i = strips(row_hot, inner_i)
    factor_r = strips(col_hot, factor[0])
    factor_i = strips(col_hot, factor[1])
    outer_r = outer_part(rows_r, factor_r) + outer_part(rows_i, factor_i)
    outer_i = outer_part(rows_i, factor_r) - outer_part(rows_r, factor_i)
    return (outer_r, outer_i)


def toeplitz(screened):
    energy_count = screened.shape[2] // 2
    position = jnp.arange(energy_count, dtype=jnp.int32)
    offsets = position[:, None] - position[None, :] + energy_count - 1
    return jnp.take(screened, offsets, axis=2)


def convolve(kernel, chosen):
    shape_in = chosen.shape
    flat = chosen.reshape(2, shape_in[1], shape_in[2], shape_in[3] * shape_in[4])
    form = "cef,cfm->cem"
    real_part = jnp.einsum(
        form, kernel[0], flat[0], preferred_element_type=jnp.float32
    ) - jnp.einsum(form, kernel[1], flat[1], preferred_element_type=jnp.float32)
    imag_part = jnp.einsum(
        form, kernel[0], flat[1], preferred_element_type=jnp.float32
    ) + jnp.einsum(form, kernel[1], flat[0], preferred_element_type=jnp.float32)
    return jnp.stack([real_part, imag_part]).astype(jnp.bfloat16).reshape(shape_in)


def per_device(
    retarded_diag, retarded_lower, retarded_upper, sigma_lesser, screened, kept, kept_count
):
    padded = with_halo(sigma_lesser, (("cell", 2),), 1)
    cell_count = sigma_lesser.shape[2]
    prev_cell = padded[:, :, 0:cell_count]
    next_cell = padded[:, :, 2 : cell_count + 2]
    per_side = ORB // SUB
    sides = jnp.arange(per_side, dtype=jnp.int32)
    row_hot = ((kept // per_side)[:, :, None] == sides[None, None, :]).astype(jnp.bfloat16)
    col_hot = ((kept % per_side)[:, :, None] == sides[None, None, :]).astype(jnp.bfloat16)
    first_r, first_i = kept_sandwich(row_hot, col_hot, retarded_diag, sigma_lesser)
    second_r, second_i = kept_sandwich(row_hot, col_hot, retarded_lower, prev_cell)
    third_r, third_i = kept_sandwich(row_hot, col_hot, retarded_upper, next_cell)
    lesser = jnp.stack([first_r + second_r + third_r, first_i + second_i + third_i]).astype(
        jnp.bfloat16
    )
    lesser = lesser.reshape(lesser.shape[:4] + (SUB * SUB,))
    live_slots = (jnp.arange(KMAX, dtype=jnp.int32)[None, :] < kept_count[:, None]).astype(
        jnp.bfloat16
    )
    chosen = lesser * live_slots[None, :, None, :, None]
    kernel = toeplitz(screened)
    mapper = partial(convolve, kernel)
    convolved = mapper(lax.all_to_all(chosen, "energy", split_axis=4, concat_axis=2, tiled=True))
    result = lax.all_to_all(convolved, "energy", split_axis=2, concat_axis=4, tiled=True)
    return jnp.swapaxes(result, 1, 2)


def solution(mesh):
    placed = (
        P(None, "energy", "cell", None, None),
        P(None, "energy", "cell", None, None),
        P(None, "energy", "cell", None, None),
        P(None, "energy", "cell", None, None),
        P(None, "cell", None),
        P("cell", None),
        P("cell"),
    )
    return jax.shard_map(
        per_device,
        mesh=mesh,
        in_specs=placed,
        out_specs=P(None, "energy", "cell", None, None),
        check_vma=False,
    )
```

profile of v0, /device:TPU:0, one launch (start us, length us, event | category | flops | bytes accessed | tf_op | source)
XLA Modules:
  0.0 200.7 jit_solution(6799111705705780635)
XLA Ops:
  0.0 1.4 fusion.119
  1.4 5.0 %collective-permute-start = (bf16[2,2,1,256,256]{4,3,2,1,0:T(8,128)(2,1)S(1)}, bf16[2,2,1,256,256]{4,3,2,1,0:T(8,128)(2,1)S(1)}, u32[]{:S(2)}, u32[]{:S(2)}) collective-permute-start(bf16[2,2,1,256,256]{4,3,2,1,0:T(8,128)(2,1)S(1)} %get-tuple-element.11), channel_id=1, source_target_pairs={{0,1},{1,2},{2,3},{4,5},{5,6},{6,7},{8,9},{9,10},{10,11},{12,13},{... | collective-permute-start | bytes 1572872 | tf_op jit(solution)/shard_map/ppermute | solution.py:18
  6.4 1.4 collective-permute-start.1
  7.8 1.7 fusion.58
  9.5 0.4 fusion.64
  10.1 0.5 copy-done.5
  10.7 0.5 add_convert_fusion.4
  11.1 0.5 subtract_convert_fusion.2
  11.6 0.9 convert_bitcast_fusion.9
  12.5 0.9 convert_bitcast_fusion.11
  13.4 1.1 convert_bitcast_fusion.8
  14.5 1.1 convert_bitcast_fusion.10
  15.7 2.2 %fusion.26 = f32[4,2,8,64,64]{4,3,2,1,0:T(8,128)} fusion(bf16[2,4,8,64,256]{4,2,3,0,1:T(8,128)(2,1)S(1)} %convert_bitcast_fusion.8, bf16[2,4,8,64,256]{4,2,3,0,1:T(8,128)(2,1)S(1)} %convert_bitcast_fusion.11), kind=kOutput, calls=%fused_computation.49 | convolution fusion | flops 134217728 | bytes 5242880 | tf_op jit(solution)/shard_map/eckij,eckqj->cekiq/dot_general | solution.py:38
  17.9 0.8 fusion.28
  18.7 0.8 copy-done.3
  19.5 0.2 fusion.118
  19.7 1.1 convert_bitcast_fusion.6
  20.8 1.1 convert_bitcast_fusion.4
  21.9 0.5 copy-done.2
  22.4 0.2 fusion.120
  22.6 1.1 convert_bitcast_fusion.2
  23.7 1.3 convert_bitcast_fusion
  25.1 0.5 constant_dynamic-update-slice_fusion
  25.6 0.4 fusion.46
  26.1 0.4 fusion.48
  26.5 0.4 subtract_convert_fusion
  27.0 0.9 convert_bitcast_fusion.3
  27.9 2.1 %fusion.2 = f32[4,2,8,64,64]{4,3,2,1,0:T(8,128)} fusion(bf16[2,4,8,64,256]{4,2,3,0,1:T(8,128)(2,1)S(1)} %convert_bitcast_fusion, bf16[2,4,8,64,256]{4,2,3,0,1:T(8,128)(2,1)S(1)} %convert_bitcast_fusion.3), kind=kOutput, calls=%fused_computation.25 | convolution fusion | flops 134217728 | bytes 5242880 | tf_op jit(solution)/shard_map/eckij,eckqj->cekiq/dot_general | solution.py:38
  30.0 0.8 fusion.10
  30.8 0.5 add_convert_fusion.2
  31.3 0.9 convert_bitcast_fusion.1
  32.2 2.1 %fusion.6 = f32[4,2,8,64,64]{4,3,2,1,0:T(8,128)} fusion(bf16[2,4,8,64,256]{4,2,3,0,1:T(8,128)(2,1)S(1)} %convert_bitcast_fusion.1, bf16[2,4,8,64,256]{4,2,3,0,1:T(8,128)(2,1)S(1)} %convert_bitcast_fusion.2), kind=kOutput, calls=%fused_computation.29 | convolution fusion | flops 134217728 | bytes 5242880 | tf_op jit(solution)/shard_map/eckij,eckqj->cekiq/dot_general | solution.py:38
  34.4 0.8 fusion.4
  35.2 0.4 fusion.52
  35.6 0.4 fusion.54
  36.1 0.4 subtract_convert_fusion.1
  36.5 0.9 convert_bitcast_fusion.7
  37.4 2.2 %fusion.14 = f32[4,2,8,64,64]{4,3,2,1,0:T(8,128)} fusion(bf16[2,4,8,64,256]{4,2,3,0,1:T(8,128)(2,1)S(1)} %convert_bitcast_fusion.4, bf16[2,4,8,64,256]{4,2,3,0,1:T(8,128)(2,1)S(1)} %convert_bitcast_fusion.7), kind=kOutput, calls=%fused_computation.37 | convolution fusion | flops 134217728 | bytes 5242880 | tf_op jit(solution)/shard_map/eckij,eckqj->cekiq/dot_general | solution.py:38
  39.6 0.8 fusion.22
  40.4 0.5 add_convert_fusion.3
  40.9 0.9 convert_bitcast_fusion.5
  41.8 2.4 %fusion.18 = f32[4,2,8,64,64]{4,3,2,1,0:T(8,128)} fusion(bf16[2,4,8,64,256]{4,2,3,0,1:T(8,128)(2,1)S(1)} %convert_bitcast_fusion.5, bf16[2,4,8,64,256]{4,2,3,0,1:T(8,128)(2,1)S(1)} %convert_bitcast_fusion.6), kind=kOutput, calls=%fused_computation.41 | convolution fusion | flops 134217728 | bytes 5242880 | tf_op jit(solution)/shard_map/eckij,eckqj->cekiq/dot_general | solution.py:38
  44.2 0.8 fusion.16
  45.0 1.3 add_convert_fusion.1
  46.3 1.6 stack.18
  47.9 6.0 %add_convert_fusion = bf16[4,2,8,64,64]{4,3,2,1,0:T(8,128)(2,1)S(1)} fusion(f32[4,2,8,64,64]{4,3,2,1,0:T(8,128)} %fusion.6, f32[4,2,8,64,64]{4,3,2,1,0:T(8,128)} %fusion.2, f32[4,2,8,64,64]{4,3,2,1,0:T(8,128)} %fusion.18, f32[4,2,8,64,64]{4,3,2,1,0:T(8,128)} %fusion.14, f32[4,2,8,64,64]{4,3,2,1,0:T(8,128)} %fusion.26, ...), kind=kOutput, calls=%fused_computation.5 | convolution fusion | flops 135790592 | bytes 9961472 | tf_op jit(solution)/shard_map/eckij,eckqj->cekiq/dot_general | solution.py:38
  53.9 0.8 stack.19
  54.7 1.2 maximum_multiply_fusion
  55.9 28.1 %copy.169 = bf16[2,4,2,8,4096]{3,2,1,0,4:T(2,128)(2,1)} copy(bf16[2,4,2,8,4096]{4,3,2,1,0:T(8,128)(2,1)S(1)} %maximum_multiply_fusion) | data formatting | bytes 2097152 | tf_op jit(solution)/shard_map/mul | solution.py:96
  84.0 20.5 %reshape.121 = bf16[8,2,32768]{2,1,0:T(2,128)(2,1)} reshape(bf16[4096,2,4,2,8]{4,3,2,1,0:T(2,128)(2,1)} %bitcast.163) | data formatting | bytes 2097152
  104.4 4.0 %all-to-all-start = ((bf16[8,2,32768]{2,1,0:T(2,128)(2,1)}), bf16[8,2,32768]{2,1,0:T(2,128)(2,1)S(1)}, u32[]{:S(2)}, u32[]{:S(2)}) async-start(bf16[8,2,32768]{2,1,0:T(2,128)(2,1)} %reshape.121), calls=%async_computation | async-start | bytes 2097152 | tf_op jit(solution)/shard_map/all_to_all | solution.py:99
  108.6 0.9 gather_fusion
  109.6 0.3 copy.176
  109.9 13.8 %all-to-all-done = bf16[8,2,32768]{2,1,0:T(2,128)(2,1)S(1)} async-done(((bf16[8,2,32768]{2,1,0:T(2,128)(2,1)}), bf16[8,2,32768]{2,1,0:T(2,128)(2,1)S(1)}, u32[]{:S(2)}, u32[]{:S(2)}) %all-to-all-start) | async-done | bytes 1048608 | tf_op jit(solution)/shard_map/all_to_all | solution.py:99
  123.7 20.6 %reshape.122 = bf16[4096,2,4,2,8]{4,3,2,1,0:T(2,128)(2,1)} reshape(bf16[8,2,32768]{2,1,0:T(2,128)(2,1)S(1)} %all-to-all-done) | data formatting | bytes 2097152
  144.3 35.2 %copy.170 = bf16[2,4,2,8,8,512]{5,3,2,4,1,0:T(8,128)(2,1)S(1)} copy(bf16[2,4,2,8,8,512]{3,2,1,0,5,4:T(2,128)(2,1)} %bitcast.164) | data formatting | bytes 2097152 | tf_op jit(solution)/shard_map/all_to_all | solution.py:99
  179.7 0.2 squeeze.77
  179.9 0.2 squeeze.79
  180.2 0.3 fusion.84
  180.4 0.3 fusion.85
  180.7 0.3 fusion.1
  181.2 0.3 fusion
  181.9 17.8 %all_to_all.33 = bf16[2,4,16,8,512]{4,3,1,0,2:T(8,128)(2,1)S(1)} all-to-all(bf16[2,4,16,8,512]{4,3,1,0,2:T(8,128)(2,1)S(1)} %copy.177), channel_id=1, replica_groups=mesh['energy'=8,'cell'=4] {'energy'}, dimensions={2} | all-to-all | bytes 2097152 | tf_op jit(solution)/shard_map/all_to_all | solution.py:100
  199.6 1.1 copy.173
  (31 shorter events, 1.2 us)
Async XLA Ops:
  0.0 7.8 %copy-start = (bf16[2,2,4,256,256]{4,3,2,1,0:T(8,128)(2,1)S(1)}, bf16[2,2,4,256,256]{4,3,2,1,0:T(8,128)(2,1)}, u32[]{:S(2)}) copy-start(bf16[2,2,4,256,256]{4,3,2,1,0:T(8,128)(2,1)} %param.10) | copy-start | bytes 6291460
  1.4 23.6 %collective-permute-start = (bf16[2,2,1,256,256]{4,3,2,1,0:T(8,128)(2,1)S(1)}, bf16[2,2,1,256,256]{4,3,2,1,0:T(8,128)(2,1)S(1)}, u32[]{:S(2)}, u32[]{:S(2)}) collective-permute-start(bf16[2,2,1,256,256]{4,3,2,1,0:T(8,128)(2,1)S(1)} %get-tuple-element.11), channel_id=1, source_target_pairs={{0,1},{1,2},{2,3},{4,5},{5,6},{6,7},{8,9},{9,10},{10,11},{12,13},{... | collective-permute-start | bytes 1572872 | tf_op jit(solution)/shard_map/ppermute | solution.py:18
  6.4 3.1 %copy-start.1 = (bf16[2,2,4,256,256]{4,3,2,1,0:T(8,128)(2,1)S(1)}, bf16[2,2,4,256,256]{4,3,2,1,0:T(8,128)(2,1)}, u32[]{:S(2)}) copy-start(bf16[2,2,4,256,256]{4,3,2,1,0:T(8,128)(2,1)} %param.7) | copy-start | bytes 6291460
  6.4 19.2 %collective-permute-start.1 = (bf16[2,2,1,256,256]{4,3,2,1,0:T(8,128)(2,1)S(1)}, bf16[2,2,1,256,256]{4,3,2,1,0:T(8,128)(2,1)S(1)}, u32[]{:S(2)}, u32[]{:S(2)}) collective-permute-start(bf16[2,2,1,256,256]{4,3,2,1,0:T(8,128)(2,1)S(1)} %get-tuple-element.12), channel_id=1, source_target_pairs={{1,0},{2,1},{3,2},{5,4},{6,5},{7,6},{9,8},{10,9},{11,10},{13,12},{... | collective-permute-start | bytes 1572872 | tf_op jit(solution)/shard_map/ppermute | solution.py:21
  10.0 0.7 copy-start.5
  12.5 5.4 %copy-start.4 = (bf16[2,4,8,64,256]{4,2,3,0,1:T(8,128)(2,1)}, bf16[2,4,8,64,256]{4,2,3,0,1:T(8,128)(2,1)S(1)}, u32[]{:S(2)}) copy-start(bf16[2,4,8,64,256]{4,2,3,0,1:T(8,128)(2,1)S(1)} %convert_bitcast_fusion.9) | copy-start | bytes 6291460
  17.9 1.6 copy-start.3
  20.8 1.6 copy-start.2
  23.7 1.3 copy-start.7
  104.4 4.1 %copy-start.6 = (bf16[2,4,32]{2,1,0:T(4,128)(2,1)S(1)}, bf16[2,4,32]{2,1,0:T(4,128)(2,1)}, u32[]{:S(2)}) copy-start(bf16[2,4,32]{2,1,0:T(4,128)(2,1)} %param.11) | copy-start | bytes 1540
  104.4 19.3 %all-to-all-start = ((bf16[8,2,32768]{2,1,0:T(2,128)(2,1)}), bf16[8,2,32768]{2,1,0:T(2,128)(2,1)S(1)}, u32[]{:S(2)}, u32[]{:S(2)}) async-start(bf16[8,2,32768]{2,1,0:T(2,128)(2,1)} %reshape.121), calls=%async_computation | async-start | bytes 2097152 | tf_op jit(solution)/shard_map/all_to_all | solution.py:99
where the time goes:
time: 202 us; the launch traced here: 201 us
  local copies, waits for them, and re-layouts  115 us (57%)
  matrix products  42.3 us (21%)
  blocking collectives  17.8 us (9%)
  waiting for transfers between devices  13.8 us (7%)
  starting transfers between devices  10.3 us (5%)
    unnamed x22, local copies, waits for them, and re-layouts  43.4 us
    all_to_all x1, local copies, waits for them, and re-layouts, per_device(): lax.all_to_all(chosen, 'energy', split_axis=4, concat_axis=2, tiled=True)  35.2 us
    mul x1, local copies, waits for them, and re-layouts, per_device(): chosen = lesser * live_slots[None, :, None, :, None]  28.1 us
    dot_general x12, matrix products, outer_part(): jnp.einsum('eckij,eckqj->cekiq', left_side, right_side, preferred_element...  22.3 us
    all_to_all x1, blocking collectives, per_device(): lax.all_to_all(convolved, 'energy', split_axis=2, concat_axis=4, tiled=True)  17.8 us
    all_to_all x1, waiting for transfers between devices, per_device(): lax.all_to_all(chosen, 'energy', split_axis=4, concat_axis=2, tiled=True)  13.8 us
    dot_general x12, matrix products, strips(): jnp.einsum('ckp,ecpij->eckij', hot, shaped, preferred_element_type=jnp.fl...  12.3 us
    dot_general x12, matrix products, batched(): jnp.einsum('ecij,ecjk->ecik', left_side, right_side, preferred_element_ty...  6.58 us
  transfers between devices with their start and end apart: 3, of which 1 were waited for; matrix products, arithmetic and copies ran while one was open for 9% of the time, Pallas kernels for 0%

commit v1 on v0

v1 whole, which is shorter than its diff:
```python
from functools import partial

import jax
import jax.numpy as jnp
from jax import lax
from jax.experimental import pallas as pl
from jax.experimental.pallas import tpu as pltpu
from jax.sharding import PartitionSpec as P

SUB = 64
LANES = 2 * SUB
PAIRS = SUB // 2
STEP = 8


def packing_order(cell_count):
    interior = list(range(1, cell_count - 1))
    return interior + [0, cell_count - 1] if cell_count > 1 else [0]


def slot_base(count_ref, order, position):
    base = jnp.int32(0)
    for place, cell in enumerate(order[:-1]):
        base = base + jnp.where(place < position, count_ref[cell], 0)
    return base


def inner_products(factor, middle_r, middle_i, out_ref):
    row = jnp.concatenate([factor[0, 0, 0], factor[1, 0, 0]], axis=1)
    real_part = jnp.dot(
        row, jnp.concatenate([middle_r, -middle_i], axis=0), preferred_element_type=jnp.float32
    )
    out_ref[0] = real_part.astype(jnp.bfloat16)
    imag_part = jnp.dot(
        row, jnp.concatenate([middle_i, middle_r], axis=0), preferred_element_type=jnp.float32
    )
    out_ref[1] = imag_part.astype(jnp.bfloat16)


def paired_rows(product_ref, slot, group):
    def rows(half, odd):
        start = half * SUB + group * 2 * STEP + odd
        return product_ref[slot, pl.ds(start, STEP, stride=2), :]

    left = lax.broadcasted_iota(jnp.int32, (STEP, LANES), 1) < SUB
    top_even, top_odd = rows(0, 0), rows(0, 1)
    low_even, low_odd = rows(1, 0), rows(1, 1)
    real_part = jnp.where(left, top_even, low_odd) + pltpu.roll(
        jnp.where(left, top_odd, low_even), SUB, 1
    )
    imag_part = jnp.where(left, low_even, -top_odd) + pltpu.roll(
        jnp.where(left, low_odd, -top_even), SUB, 1
    )
    return real_part, imag_part


def lesser_kernel(order, first, devices, kept_ref, count_ref, *refs):
    if first:
        diag, lower, upper, own, prev, after, out_ref, inner, product, staged = refs
        prev_r, prev_i = prev[0, 0, 0], prev[1, 0, 0]
        next_r, next_i = after[0, 0, 0], after[1, 0, 0]
    else:
        (diag, lower, upper, own, near, low, high, earlier, out_ref, inner, product, staged, sides) = refs
    place, energy = pl.program_id(0), pl.program_id(1)
    energies = pl.num_programs(1)
    cell_count = len(order)
    if first:
        position = place
        cell = place + 1
    else:
        position = place + cell_count - 2
        cell = place * (cell_count - 1)

        @pl.when((place == 0) & (energy == 0))
        def _():
            out_ref[...] = earlier[...]

        @pl.when(place == 0)
        def _():
            sides[0] = low[:, 0, 0]
            sides[1] = near[:, 0, 0]

        @pl.when(place != 0)
        def _():
            sides[0] = near[:, 0, 0]
            sides[1] = high[:, 0, 0]

        prev_r, prev_i = sides[0, 0], sides[0, 1]
        next_r, next_i = sides[1, 0], sides[1, 1]
    base = slot_base(count_ref, order, position)
    inner_products(diag, own[0, 0, 0], own[1, 0, 0], inner.at[0])
    inner_products(lower, prev_r, prev_i, inner.at[1])
    inner_products(upper, next_r, next_i, inner.at[2])
    slots = kept_ref.shape[1]
    per_side = diag.shape[3] // SUB
    tile_rows = out_ref.shape[2]
    share = PAIRS // devices
    for slot in range(slots):
        number = kept_ref[cell, slot]
        top = pl.multiple_of((number // per_side) * SUB, SUB)
        side = pl.multiple_of((number % per_side) * SUB, SUB)
        left_parts = []
        right_parts = []
        for term, factor in enumerate((diag, lower, upper)):
            size = inner.shape[-1]
            left_parts.append(inner[term, :, pl.ds(top, SUB), :].reshape(LANES, size))
            right_parts.append(factor[:, 0, 0, pl.ds(side, SUB), :].reshape(LANES, size))
        product[slot] = lax.dot_general(
            jnp.concatenate(left_parts, axis=1),
            jnp.concatenate(right_parts, axis=1),
            (((1,), (1,)), ((), ())),
            preferred_element_type=jnp.float32,
        )
        for group in range(PAIRS // STEP):
            pair = paired_rows(product, slot, group)
            device = (group * STEP) % devices
            for part in range(2):
                start = device * tile_rows + (energy * 2 + part) * share + group * STEP // devices
                staged[slot, pl.ds(start, STEP, stride=tile_rows), :] = pair[part]

    @pl.when(energy == energies - 1)
    def _():
        for slot in range(slots):
            tiles = staged[slot].reshape(devices, tile_rows, LANES)
            out_ref[:, base + slot] = tiles.astype(jnp.bfloat16)


def chosen_packed(blocks, halo, kept, kept_count, devices):
    diag, lower, upper, sigma = blocks
    low, high = halo
    _, energies, cells, size, _ = diag.shape
    slots = kept.shape[1]
    order = packing_order(cells)
    tile_rows = energies * 2 * (PAIRS // devices)
    packed = (devices, cells * slots, tile_rows, LANES)
    block = (2, 1, 1, size, size)
    whole = pl.BlockSpec(packed, lambda i, e, *_: (0, 0, 0, 0))
    scratch = [
        pltpu.VMEM((3, 2, size, size), jnp.bfloat16),
        pltpu.VMEM((slots, LANES, LANES), jnp.float32),
        pltpu.VMEM((slots, devices * tile_rows, LANES), jnp.float32),
    ]

    def call(first, places, in_specs, extra, args):
        return pl.pallas_call(
            partial(lesser_kernel, order, first, devices),
            grid_spec=pltpu.PrefetchScalarGridSpec(
                num_scalar_prefetch=2,
                grid=(places, energies),
                in_specs=in_specs,
                out_specs=whole,
                scratch_shapes=scratch + extra,
            ),
            out_shape=jax.ShapeDtypeStruct(packed, jnp.bfloat16),
            compiler_params=pltpu.CompilerParams(vmem_limit_bytes=48 << 20),
            cost_estimate=pl.CostEstimate(
                flops=places * energies * 48 * size**3, bytes_accessed=places * energies * 6 * size * size * 4, transcendentals=0
            ),
        )(kept, kept_count, *args)

    def at(cell_of):
        return pl.BlockSpec(block, lambda i, e, *_: (0, e, cell_of(i), 0, 0))

    inside = at(lambda i: i + 1)
    first_part = call(
        True,
        cells - 2,
        [inside, inside, inside, inside, at(lambda i: i), at(lambda i: i + 2)],
        [],
        (diag, lower, upper, sigma, sigma, sigma),
    )
    outside = at(lambda i: i * (cells - 1))
    near = at(lambda i: 1 + i * (cells - 3))
    only = at(lambda i: 0)
    return call(
        False,
        2,
        [outside, outside, outside, outside, near, only, only, whole],
        [pltpu.VMEM((2, 2, size, size), jnp.bfloat16)],
        (diag, lower, upper, sigma, sigma, low, high, first_part),
    )


def mixing_kernel(cells, share, screened_ref, weight_ref, table):
    doubled = screened_ref.shape[1] // 2
    total = doubled // 2
    lane_count = table.shape[2]
    shape = (2 * doubled, lane_count)
    source = lax.broadcasted_iota(jnp.int32, shape, 0)
    lane = lax.broadcasted_iota(jnp.int32, shape, 1)
    offset = 2 * total - 2 - lane // (2 * share)
    part = (lane // share) % 2
    spot = lane % share
    for row in range(2 * share):
        own_part, own_spot = row // share, row % share
        wanted = jnp.where(part == own_part, 0, doubled) + offset
        sign = jnp.where(part > own_part, -1.0, 1.0)
        pick = jnp.where((source == wanted) & (spot == own_spot) & (offset >= 0), sign, 0.0)
        table[:, row, :] = jnp.dot(
            screened_ref[...], pick.astype(jnp.bfloat16), preferred_element_type=jnp.float32
        )
    size = weight_ref.shape[1]
    rows = 2 * share
    for cell in range(cells):
        for energy in range(total):
            start = (total - 1 - energy) * rows
            weight_ref[cell, energy * rows : (energy + 1) * rows, :] = table[
                cell, :, start : start + size
            ].astype(jnp.bfloat16)


def mixing_matrix(screened, devices):
    _, cells, doubled = screened.shape
    share = PAIRS // devices
    size = doubled * share
    return pl.pallas_call(
        partial(mixing_kernel, cells, share),
        out_shape=jax.ShapeDtypeStruct((cells, size, size), jnp.bfloat16),
        scratch_shapes=[pltpu.VMEM((cells, 2 * share, 2 * size), jnp.float32)],
        compiler_params=pltpu.CompilerParams(vmem_limit_bytes=48 << 20),
        cost_estimate=pl.CostEstimate(flops=1 << 20, bytes_accessed=1 << 20, transcendentals=0),
    )(jnp.concatenate([screened[0], screened[1]], axis=1))


def mix_kernel(order, group, count_ref, weight_ref, x_ref, y_ref):
    devices, _, tile_rows, _ = x_ref.shape
    ends = []
    end = jnp.int32(0)
    for cell in order[:-1]:
        end = end + count_ref[cell]
        ends.append(end)
    for slot in range(group):
        number = pl.program_id(0) * group + slot
        place = jnp.int32(0)
        for end in ends:
            place = place + jnp.where(number >= end, 1, 0)
        cell = jnp.int32(order[-1])
        for index, name in enumerate(order[:-1]):
            cell = jnp.where(place == index, name, cell)
        entries = x_ref[:, slot].reshape(devices * tile_rows, LANES)
        mixed = jnp.dot(weight_ref[cell], entries, preferred_element_type=jnp.float32)
        y_ref[:, slot] = mixed.astype(jnp.bfloat16).reshape(devices, tile_rows, LANES)


def mix(packed, weights, kept_count):
    devices, total, tile_rows, _ = packed.shape
    group = min(8, total)
    block = pl.BlockSpec((devices, group, tile_rows, LANES), lambda i, *_: (0, i, 0, 0))
    return pl.pallas_call(
        partial(mix_kernel, packing_order(kept_count.shape[0]), group),
        grid_spec=pltpu.PrefetchScalarGridSpec(
            num_scalar_prefetch=1,
            grid=(total // group,),
            in_specs=[pl.BlockSpec(weights.shape, lambda i, *_: (0, 0, 0)), block],
            out_specs=block,
        ),
        out_shape=jax.ShapeDtypeStruct(packed.shape, jnp.bfloat16),
        compiler_params=pltpu.CompilerParams(vmem_limit_bytes=48 << 20),
    )(kept_count, weights, packed)


def unpack_kernel(order, count_ref, y_ref, out_ref, rows):
    devices, total, tile_rows, _ = y_ref.shape
    _, energies, _, slots, _ = out_ref.shape
    cell = pl.program_id(0)
    position = jnp.int32(0)
    for index, name in enumerate(order):
        position = jnp.where(cell == name, index, position)
    base = slot_base(count_ref, order, position)
    for slot in range(slots):
        number = jnp.minimum(base + slot, total - 1)
        rows[:, pl.ds(slot * tile_rows, tile_rows), :] = y_ref[:, number].astype(jnp.float32)
    live = lax.broadcasted_iota(jnp.int32, (slots, LANES), 0) < count_ref[cell]
    share = PAIRS // devices
    for part in range(2):
        for energy in range(energies):
            for index in range(PAIRS):
                row = (energy * 2 + part) * share + index // devices
                entries = rows[index % devices, pl.ds(row, slots, stride=tile_rows), :]
                out_ref[part, energy, 0, :, index * LANES : (index + 1) * LANES] = jnp.where(
                    live, entries, 0.0
                ).astype(jnp.bfloat16)


def unpack(packed, kept_count, energies, slots):
    devices, total, tile_rows, _ = packed.shape
    cells = kept_count.shape[0]
    shape = (2, energies, cells, slots, SUB * SUB)
    return pl.pallas_call(
        partial(unpack_kernel, packing_order(cells)),
        grid_spec=pltpu.PrefetchScalarGridSpec(
            num_scalar_prefetch=1,
            grid=(cells,),
            in_specs=[pl.BlockSpec(packed.shape, lambda i, *_: (0, 0, 0, 0))],
            out_specs=pl.BlockSpec(
                (2, energies, 1, slots, SUB * SUB), lambda i, *_: (0, 0, i, 0, 0)
            ),
            scratch_shapes=[pltpu.VMEM((devices, slots * tile_rows, LANES), jnp.float32)],
        ),
        out_shape=jax.ShapeDtypeStruct(shape, jnp.bfloat16),
        compiler_params=pltpu.CompilerParams(vmem_limit_bytes=48 << 20),
    )(kept_count, packed)


def per_device(diag, lower, upper, sigma, screened, kept, kept_count):
    count = lax.axis_size("cell")
    devices = lax.axis_size("energy")
    forward = [(i, i + 1) for i in range(count - 1)]
    backward = [(target, source) for source, target in forward]
    low = lax.ppermute(sigma[:, :, -1:], "cell", forward)
    high = lax.ppermute(sigma[:, :, :1], "cell", backward)
    packed = chosen_packed((diag, lower, upper, sigma), (low, high), kept, kept_count, devices)
    weights = mixing_matrix(screened, devices)
    exchange = partial(lax.all_to_all, axis_name="energy", split_axis=0, concat_axis=0, tiled=True)
    mixed = mix(exchange(packed), weights, kept_count)
    return unpack(exchange(mixed), kept_count, sigma.shape[1], kept.shape[1])


def solution(mesh):
    placed = (
        P(None, "energy", "cell", None, None),
        P(None, "energy", "cell", None, None),
        P(None, "energy", "cell", None, None),
        P(None, "energy", "cell", None, None),
        P(None, "cell", None),
        P("cell", None),
        P("cell"),
    )
    return jax.shard_map(
        per_device,
        mesh=mesh,
        in_specs=placed,
        out_specs=P(None, "energy", "cell", None, None),
        check_vma=False,
    )
```

time: 202 us -> 71.7 us (0.35)
  local copies, waits for them, and re-layouts: 115 us -> 3.02 us
  matrix products: 42.3 us -> 0 us
  Pallas kernels: 0 us -> 20 us
  waiting for transfers between devices: 13.8 us -> 20.2 us
    dot_general x40 -> x0, matrix products: 42.3 us -> none  [the longest x12 22.3 us: outer_part(): jnp.einsum('eckij,eckqj->cekiq', left_side, right_side, preferred_element...]
    unnamed x22 -> x10, local copies, waits for them, and re-layouts: 43.4 us -> 1.6 us
    all_to_all x2 -> x0, local copies, waits for them, and re-layouts: 36.3 us -> none  [the longest x1 35.2 us: per_device(): lax.all_to_all(chosen, 'energy', split_axis=4, concat_axis=2, tiled=True)]
    mul x1 -> x0, local copies, waits for them, and re-layouts: 28.1 us -> none  [per_device(): chosen = lesser * live_slots[None, :, None, :, None]]
    pallas_call x0 -> x5, Pallas kernels: none -> 20 us  [the longest x2 15.4 us: call(): pl.pallas_call(partial(lesser_kernel, order, first, devices), grid_spec=p...]
    ppermute x2, waiting for transfers between devices: 0.01 us -> 5.22 us  [the longest x1 4.15 us: per_device(): high = lax.ppermute(sigma[:, :, :1], 'cell', backward)]
    another operation x3 -> x0, local copies, waits for them, and re-layouts: 2.55 us -> none  [the longest x2 2.42 us: per_device(): jnp.stack([first_r + second_r + third_r, first_i + second_i + third_i])]
  transfers between devices with their start and end apart: 3 -> 3, of which waited for: 1 -> 3; matrix products, arithmetic and copies ran while one was open for 9% -> 0% of each run, Pallas kernels for 0% -> 10%
where the time goes in v1:
time: 71.7 us; the launch traced here: 71.3 us
  waiting for transfers between devices  20.2 us (28%)
  Pallas kernels  20 us (28%)
  blocking collectives  17.8 us (25%)
  starting transfers between devices  10.1 us (14%)
  local copies, waits for them, and re-layouts  3.02 us (4%)
    all_to_all x1, blocking collectives, per_device(): return unpack(exchange(mixed), kept_count, sigma.shape[1], kept.shape[1])  17.8 us
    pallas_call x2, Pallas kernels, call(): pl.pallas_call(partial(lesser_kernel, order, first, devices), grid_spec=p...  15.4 us
    all_to_all x1, waiting for transfers between devices, per_device(): mixed = mix(exchange(packed), weights, kept_count)  15 us
    ppermute x1, starting transfers between devices, per_device(): low = lax.ppermute(sigma[:, :, -1:], 'cell', forward)  4.97 us
    ppermute x1, waiting for transfers between devices, per_device(): high = lax.ppermute(sigma[:, :, :1], 'cell', backward)  4.15 us
    all_to_all x1, starting transfers between devices, per_device(): mixed = mix(exchange(packed), weights, kept_count)  3.85 us
    pallas_call x1, Pallas kernels, unpack(): pl.pallas_call(partial(unpack_kernel, packing_order(cells)), grid_spec=pl...  2.68 us
    unnamed x10, local copies, waits for them, and re-layouts  1.6 us
  transfers between devices with their start and end apart: 3, of which 3 were waited for; matrix products, arithmetic and copies ran while one was open for 0% of the time, Pallas kernels for 10%

profile of v1, /device:TPU:0, one launch (start us, length us, event | category | flops | bytes accessed | tf_op | source)
XLA Modules:
  0.0 71.3 jit_solution(15788083476140068913)
XLA Ops:
  0.0 0.0 copy-start.2
  0.0 0.0 copy-start.3
  0.0 0.0 copy-start
  0.0 1.4 %fusion = (bf16[2,2,1,256,256]{4,3,2,1,0:T(8,128)(2,1)S(1)}, bf16[2,2,1,256,256]{4,3,2,1,0:T(8,128)(2,1)S(1)}) fusion(bf16[2,2,4,256,256]{4,3,2,1,0:T(8,128)(2,1)} %refs_4_.3), kind=kLoop, calls=%fused_computation.3 | loop fusion | bytes 2097152 | tf_op jit(solution)/shard_map/slice | solution.py:311
  1.4 5.0 %collective-permute-start = (bf16[2,2,1,256,256]{4,3,2,1,0:T(8,128)(2,1)S(1)}, bf16[2,2,1,256,256]{4,3,2,1,0:T(8,128)(2,1)S(1)}, u32[]{:S(2)}, u32[]{:S(2)}) collective-permute-start(bf16[2,2,1,256,256]{4,3,2,1,0:T(8,128)(2,1)S(1)} %get-tuple-element.6), channel_id=1, source_target_pairs={{0,1},{1,2},{2,3},{4,5},{5,6},{6,7},{8,9},{9,10},{10,11},{12,13},{... | collective-permute-start | bytes 1572872 | tf_op jit(solution)/shard_map/ppermute | solution.py:310
  6.4 1.3 %collective-permute-start.1 = (bf16[2,2,1,256,256]{4,3,2,1,0:T(8,128)(2,1)S(1)}, bf16[2,2,1,256,256]{4,3,2,1,0:T(8,128)(2,1)S(1)}, u32[]{:S(2)}, u32[]{:S(2)}) collective-permute-start(bf16[2,2,1,256,256]{4,3,2,1,0:T(8,128)(2,1)S(1)} %get-tuple-element.5), channel_id=1, source_target_pairs={{1,0},{2,1},{3,2},{5,4},{6,5},{7,6},{9,8},{10,9},{11,10},{13,12},{... | collective-permute-start | bytes 1572872 | tf_op jit(solution)/shard_map/ppermute | solution.py:311
  7.7 0.0 copy-done.2
  7.7 0.0 copy-done.3
  7.7 0.0 copy-done
  7.7 0.0 copy-start.1
  7.8 1.6 %copy-done.1 = bf16[2,2,4,256,256]{4,3,2,1,0:T(8,128)(2,1)S(1)} copy-done((bf16[2,2,4,256,256]{4,3,2,1,0:T(8,128)(2,1)S(1)}, bf16[2,2,4,256,256]{4,3,2,1,0:T(8,128)(2,1)}, u32[]{:S(2)}) %copy-start.1) | copy-done | bytes 2097176
  9.3 7.1 %shard_map.74.refs_7_ = bf16[8,32,16,128]{3,2,1,0:T(8,128)(2,1)S(1)} custom-call(s32[4,8]{1,0:T(4,128)S(1)} %copy-done.2, s32[4]{0:T(128)S(1)} %copy-done.3, bf16[2,2,4,256,256]{4,3,2,1,0:T(8,128)(2,1)S(1)} %copy-done, bf16[2,2,4,256,256]{4,3,2,1,0:T(8,128)(2,1)S(1)} %copy-done.1, bf16[2,2,4,256,256]{4,3,2,1,0:T(8,128)(2,1)} %refs_2_.3, ...), custom_call_target="tpu_custom_call" | custom-call | flops 3221225472 | bytes 6291456 | tf_op jit(solution)/shard_map/pallas_call | solution.py:145
  16.5 1.1 %collective-permute-done.refs_5_ = bf16[2,2,1,256,256]{4,3,2,1,0:T(8,128)(2,1)S(1)} collective-permute-done((bf16[2,2,1,256,256]{4,3,2,1,0:T(8,128)(2,1)S(1)}, bf16[2,2,1,256,256]{4,3,2,1,0:T(8,128)(2,1)S(1)}, u32[]{:S(2)}, u32[]{:S(2)}) %collective-permute-start) | collective-permute-done | bytes 524320 | tf_op jit(solution)/shard_map/ppermute | solution.py:310
  17.5 4.1 %collective-permute-done.1.refs_6_ = bf16[2,2,1,256,256]{4,3,2,1,0:T(8,128)(2,1)S(1)} collective-permute-done((bf16[2,2,1,256,256]{4,3,2,1,0:T(8,128)(2,1)S(1)}, bf16[2,2,1,256,256]{4,3,2,1,0:T(8,128)(2,1)S(1)}, u32[]{:S(2)}, u32[]{:S(2)}) %collective-permute-start.1) | collective-permute-done | bytes 524320 | tf_op jit(solution)/shard_map/ppermute | solution.py:311
  21.7 8.3 %shard_map.75 = bf16[8,32,16,128]{3,2,1,0:T(8,128)(2,1)} custom-call(s32[4,8]{1,0:T(4,128)S(1)} %copy-done.2, s32[4]{0:T(128)S(1)} %copy-done.3, bf16[2,2,4,256,256]{4,3,2,1,0:T(8,128)(2,1)S(1)} %copy-done, bf16[2,2,4,256,256]{4,3,2,1,0:T(8,128)(2,1)} %refs_1_.3, bf16[2,2,4,256,256]{4,3,2,1,0:T(8,128)(2,1)} %refs_2_.3, bf16[2,2,4,256,256]{4,3,2,1,0:T(8,128)(2,1)} %refs_4_.3, ...), custom_call_target="tpu_custom_call" | custom-call | flops 3221225472 | bytes 6291456 | tf_op jit(solution)/shard_map/pallas_call | solution.py:145
  30.0 0.0 copy-start.4
  30.0 3.9 %all-to-all-start = ((bf16[8,32,16,128]{3,2,1,0:T(8,128)(2,1)}), bf16[8,32,16,128]{3,2,1,0:T(8,128)(2,1)S(1)}, u32[]{:S(2)}, u32[]{:S(2)}) async-start(bf16[8,32,16,128]{3,2,1,0:T(8,128)(2,1)} %shard_map.75), calls=%async_computation | async-start | bytes 2097152 | tf_op jit(solution)/shard_map/all_to_all | solution.py:315
  33.9 0.0 copy-done.4
  33.9 0.1 pad_maximum_fusion.screened_ref
  34.0 0.3 shard_map.73.weight_ref
  34.3 15.0 %all-to-all-done.x_ref = bf16[8,32,16,128]{3,2,1,0:T(8,128)(2,1)S(1)} async-done(((bf16[8,32,16,128]{3,2,1,0:T(8,128)(2,1)}), bf16[8,32,16,128]{3,2,1,0:T(8,128)(2,1)S(1)}, u32[]{:S(2)}, u32[]{:S(2)}) %all-to-all-start) | async-done | bytes 1048608 | tf_op jit(solution)/shard_map/all_to_all | solution.py:315
  49.3 1.6 %shard_map.76 = bf16[8,32,16,128]{3,2,1,0:T(8,128)(2,1)S(1)} custom-call(s32[4]{0:T(128)S(1)} %copy-done.3, bf16[4,128,128]{2,1,0:T(8,128)(2,1)S(1)} %shard_map.73.weight_ref, bf16[8,32,16,128]{3,2,1,0:T(8,128)(2,1)S(1)} %all-to-all-done.x_ref), custom_call_target="tpu_custom_call" | custom-call | tf_op jit(solution)/shard_map/pallas_call | solution.py:249
  50.9 17.8 %all_to_all.10.y_ref = bf16[8,32,16,128]{3,2,1,0:T(8,128)(2,1)S(1)} all-to-all(bf16[8,32,16,128]{3,2,1,0:T(8,128)(2,1)S(1)} %shard_map.76), channel_id=1, replica_groups=mesh['energy'=8,'cell'=4] {'energy'}, dimensions={0} | all-to-all | bytes 2097152 | tf_op jit(solution)/shard_map/all_to_all | solution.py:316
  68.7 2.7 %shard_map.77 = bf16[2,2,4,8,4096]{4,3,2,1,0:T(8,128)(2,1)} custom-call(s32[4]{0:T(128)S(1)} %copy-done.3, bf16[8,32,16,128]{3,2,1,0:T(8,128)(2,1)S(1)} %all_to_all.10.y_ref), custom_call_target="tpu_custom_call" | custom-call | tf_op jit(solution)/shard_map/pallas_call | solution.py:289
  (1 shorter events, 0.0 us)
Async XLA Ops:
  0.0 7.7 %copy-start.2 = (s32[4,8]{1,0:T(4,128)S(1)}, s32[4,8]{1,0:T(4,128)}, u32[]{:S(2)}) copy-start(s32[4,8]{1,0:T(4,128)} %kept_ref.3) | copy-start | bytes 388
  0.0 7.7 %copy-start.3 = (s32[4]{0:T(128)S(1)}, s32[4]{0:T(128)}, u32[]{:S(2)}) copy-start(s32[4]{0:T(128)} %count_ref.7) | copy-start | bytes 52
  0.0 7.7 %copy-start = (bf16[2,2,4,256,256]{4,3,2,1,0:T(8,128)(2,1)S(1)}, bf16[2,2,4,256,256]{4,3,2,1,0:T(8,128)(2,1)}, u32[]{:S(2)}) copy-start(bf16[2,2,4,256,256]{4,3,2,1,0:T(8,128)(2,1)} %refs_0_.3) | copy-start | bytes 6291460
  1.4 16.1 %collective-permute-start = (bf16[2,2,1,256,256]{4,3,2,1,0:T(8,128)(2,1)S(1)}, bf16[2,2,1,256,256]{4,3,2,1,0:T(8,128)(2,1)S(1)}, u32[]{:S(2)}, u32[]{:S(2)}) collective-permute-start(bf16[2,2,1,256,256]{4,3,2,1,0:T(8,128)(2,1)S(1)} %get-tuple-element.6), channel_id=1, source_target_pairs={{0,1},{1,2},{2,3},{4,5},{5,6},{6,7},{8,9},{9,10},{10,11},{12,13},{... | collective-permute-start | bytes 1572872 | tf_op jit(solution)/shard_map/ppermute | solution.py:310
  6.4 15.3 %collective-permute-start.1 = (bf16[2,2,1,256,256]{4,3,2,1,0:T(8,128)(2,1)S(1)}, bf16[2,2,1,256,256]{4,3,2,1,0:T(8,128)(2,1)S(1)}, u32[]{:S(2)}, u32[]{:S(2)}) collective-permute-start(bf16[2,2,1,256,256]{4,3,2,1,0:T(8,128)(2,1)S(1)} %get-tuple-element.5), channel_id=1, source_target_pairs={{1,0},{2,1},{3,2},{5,4},{6,5},{7,6},{9,8},{10,9},{11,10},{13,12},{... | collective-permute-start | bytes 1572872 | tf_op jit(solution)/shard_map/ppermute | solution.py:311
  7.7 1.6 %copy-start.1 = (bf16[2,2,4,256,256]{4,3,2,1,0:T(8,128)(2,1)S(1)}, bf16[2,2,4,256,256]{4,3,2,1,0:T(8,128)(2,1)}, u32[]{:S(2)}) copy-start(bf16[2,2,4,256,256]{4,3,2,1,0:T(8,128)(2,1)} %refs_1_.3) | copy-start | bytes 6291460
  30.0 3.9 %copy-start.4 = (bf16[2,4,32]{2,1,0:T(4,128)(2,1)S(1)}, bf16[2,4,32]{2,1,0:T(4,128)(2,1)}, u32[]{:S(2)}) copy-start(bf16[2,4,32]{2,1,0:T(4,128)(2,1)} %param.11) | copy-start | bytes 1540
  30.0 19.3 %all-to-all-start = ((bf16[8,32,16,128]{3,2,1,0:T(8,128)(2,1)}), bf16[8,32,16,128]{3,2,1,0:T(8,128)(2,1)S(1)}, u32[]{:S(2)}, u32[]{:S(2)}) async-start(bf16[8,32,16,128]{3,2,1,0:T(8,128)(2,1)} %shard_map.75), calls=%async_computation | async-start | bytes 2097152 | tf_op jit(solution)/shard_map/all_to_all | solution.py:315
